TPU v7x, 128 devices: a whole 4x4x4 slice. The times are simulated.
128 devices in a mesh: subset: 8 (over z, y_hi), tile: 16 (over x, y_lo, core).
Axes of the slice: x: 4, y: 4 (y_hi: 2, y_lo: 2; y = y_hi * 2 + y_lo), z: 4, core: 2. Of those that a mesh axis runs over, the one named last changes fastest.
Arguments:
- start_volume: float32 [16384, 2048], P('tile', 'subset'), may hold values from 0 to 2
- tiles: bfloat16 [8, 128, 8, 128, 128], P('subset', 'tile'), may hold values from 5e-05 to 30
- pattern: int32 [8, 128, 8], P('subset', 'tile'), may hold values from 0 to 15, as said below
- projections: float32 [8, 2048, 2048], P('subset', 'tile'), may hold values from 0.5 to 1.5
Outputs:
- volume: float32 [16384, 2048], P('tile', 'subset')
Inputs may be any that keep to these rules, and one draw needn't show every extreme that they name: `pattern`: for each subset and pixel block the 8 ray blocks differ; in each subset every ray block is named by some pixel block.
All inputs are finite; a program needn't handle non-finite values.
Results may differ from a plain program's by a relative error of at most 0.00031.
Values may be sent and summed in bfloat16 or wider, within the bound.
A program may use at most 64 MiB of HBM per device.

v0:
```python
import jax
import jax.numpy as jnp
from jax import lax
from jax.sharding import PartitionSpec as P

ITERS = 1


def passed_along(value, axis, by):
    devices = lax.axis_size(axis)
    return lax.ppermute(value, axis, [(i, (i + by) % devices) for i in range(devices)])


def per_device(start_volume, tiles, pattern, projections):
    tile_set = tiles[0]
    links = pattern[0]
    flat_links = links.reshape(-1)
    block = tile_set.shape[-1]
    ray_blocks = lax.axis_size("tile")
    subset_count = lax.axis_size("subset")
    my_subset = lax.axis_index("subset")
    columns = start_volume.shape[1]
    row_part = (
        jnp.zeros((ray_blocks, block), jnp.float32)
        .at[flat_links]
        .add(jnp.sum(tile_set, axis=-1, dtype=jnp.float32).reshape(-1, block))
    )
    ray_weight = lax.psum_scatter(row_part, "tile", scatter_dimension=0, tiled=True)
    pixel_weight = jnp.sum(tile_set, axis=(1, 2), dtype=jnp.float32).reshape(-1, 1)

    def update(panel, start):
        width = panel.shape[1]
        image = panel.astype(jnp.bfloat16).reshape(-1, block, width)
        contrib = jnp.einsum("qkrp,qps->qkrs", tile_set, image, preferred_element_type=jnp.float32)
        partial_sums = (
            jnp.zeros((ray_blocks, block, width), jnp.float32)
            .at[flat_links]
            .add(contrib.reshape(-1, block, width))
        )
        measured = lax.dynamic_slice_in_dim(projections[0], start, width, 1)[None]
        own_sums = lax.psum_scatter(partial_sums, "tile", scatter_dimension=0, tiled=True)
        residual = (measured - own_sums / ray_weight[:, :, None]).astype(jnp.bfloat16)
        residual_all = lax.all_gather(residual, "tile", axis=0, tiled=True)
        chosen = residual_all[links]
        correction = jnp.einsum(
            "qkrp,qkrs->qps", tile_set, chosen, preferred_element_type=jnp.float32
        )
        return panel + 0.9 * correction.reshape(-1, width) / pixel_weight

    def advance(panel):
        return passed_along(panel, "subset", 1)

    def section(step, volume):
        anchor = jnp.mod(my_subset - step, subset_count)
        start = anchor * columns
        return advance(update(volume, start))

    return lax.fori_loop(0, ITERS * subset_count, section, start_volume)


def solution(mesh):
    in_specs = (
        P("tile", "subset"),
        P("subset", "tile", None, None, None),
        P("subset", "tile", None),
        P("subset", "tile", None),
    )
    out_specs = P("tile", "subset")
    return jax.shard_map(
        per_device, mesh=mesh, in_specs=in_specs, out_specs=out_specs, check_vma=False
    )
```

profile of v0, /device:TPU:1, one launch (start us, length us, event | category | flops | bytes accessed | tf_op | source)
XLA Modules:
  0.0 1258.9 jit_solution(12946721996703813403)
XLA Ops:
  11.1 28.5 %all-reduce = f32[16,128]{1,0:T(8,128)S(1)} all-reduce(f32[16,128]{1,0:T(8,128)S(1)} %scatter_custom_fusion.1), channel_id=3, replica_groups=mesh['subset'=8,'tile'=16] {'tile'}, use_global_device_ids=true, to_apply=%region_2.0.clone | all-reduce | flops 2048 | bytes 16384
  41.0 1210.4 %while.15 = (s32[]{:T(128)}, f32[1024,256]{1,0:T(8,128)S(1)}, s32[]{:T(128)}, f32[1,128,2048]{2,1,0:T(8,128)}, s32[64]{0:T(128)S(1)}, /*index=5*/bf16[8,8,128,12...) while((s32[]{:T(128)}, f32[1024,256]{1,0:T(8,128)S(1)}, ...), condition=%wide.region_7.8_spmd, body=%wide.region_4.7_spmd.sunk | while | flops 1076987264 | bytes 98446600 | solution.py:58
  59.8 63.2 %reduce-scatter.2.cloned.1.call-done = f32[1,128,256]{2,1,0:T(8,128)} async-done(((f32[16,128,256]{2,1,0:T(8,128)}), f32[1,128,256]{2,1,0:T(8,128)}) %reduce-scatter.2.cloned.1.call-update) | async-done | bytes 131088 | tf_op jit(solution)/shard_map/while/body/eval_jaxpr/reduce_scatter | solution.py:41
  124.7 34.8 %all-gather.2.cloned.1.call-done = bf16[16,128,256]{2,1,0:T(8,128)(2,1)} async-done(((bf16[1,128,256]{2,1,0:T(8,128)(2,1)}), bf16[16,128,256]{2,1,0:T(8,128)(2,1)}) %all-gather.2.cloned.1.call-update) | async-done | bytes 1048592 | tf_op jit(solution)/shard_map/while/body/eval_jaxpr/all_gather | solution.py:43
  170.3 25.8 %collective-permute-done = f32[1024,256]{1,0:T(8,128)S(1)} collective-permute-done((f32[1024,256]{1,0:T(8,128)}, f32[1024,256]{1,0:T(8,128)S(1)}, u32[]{:S(2)}, u32[]{:S(2)}) %collective-permute-start) | collective-permute-done | bytes 1048608 | tf_op jit(solution)/shard_map/while/body/eval_jaxpr/ppermute | solution.py:11
  214.9 59.0 %reduce-scatter.2.cloned.1.call-done = f32[1,128,256]{2,1,0:T(8,128)} async-done(((f32[16,128,256]{2,1,0:T(8,128)}), f32[1,128,256]{2,1,0:T(8,128)}) %reduce-scatter.2.cloned.1.call-update) | async-done | bytes 131088 | tf_op jit(solution)/shard_map/while/body/eval_jaxpr/reduce_scatter | solution.py:41
  275.7 34.7 %all-gather.2.cloned.1.call-done = bf16[16,128,256]{2,1,0:T(8,128)(2,1)} async-done(((bf16[1,128,256]{2,1,0:T(8,128)(2,1)}), bf16[16,128,256]{2,1,0:T(8,128)(2,1)}) %all-gather.2.cloned.1.call-update) | async-done | bytes 1048592 | tf_op jit(solution)/shard_map/while/body/eval_jaxpr/all_gather | solution.py:43
  321.1 25.8 %collective-permute-done = f32[1024,256]{1,0:T(8,128)S(1)} collective-permute-done((f32[1024,256]{1,0:T(8,128)}, f32[1024,256]{1,0:T(8,128)S(1)}, u32[]{:S(2)}, u32[]{:S(2)}) %collective-permute-start) | collective-permute-done | bytes 1048608 | tf_op jit(solution)/shard_map/while/body/eval_jaxpr/ppermute | solution.py:11
  365.6 58.8 %reduce-scatter.2.cloned.1.call-done = f32[1,128,256]{2,1,0:T(8,128)} async-done(((f32[16,128,256]{2,1,0:T(8,128)}), f32[1,128,256]{2,1,0:T(8,128)}) %reduce-scatter.2.cloned.1.call-update) | async-done | bytes 131088 | tf_op jit(solution)/shard_map/while/body/eval_jaxpr/reduce_scatter | solution.py:41
  426.3 34.8 %all-gather.2.cloned.1.call-done = bf16[16,128,256]{2,1,0:T(8,128)(2,1)} async-done(((bf16[1,128,256]{2,1,0:T(8,128)(2,1)}), bf16[16,128,256]{2,1,0:T(8,128)(2,1)}) %all-gather.2.cloned.1.call-update) | async-done | bytes 1048592 | tf_op jit(solution)/shard_map/while/body/eval_jaxpr/all_gather | solution.py:43
  471.8 25.8 %collective-permute-done = f32[1024,256]{1,0:T(8,128)S(1)} collective-permute-done((f32[1024,256]{1,0:T(8,128)}, f32[1024,256]{1,0:T(8,128)S(1)}, u32[]{:S(2)}, u32[]{:S(2)}) %collective-permute-start) | collective-permute-done | bytes 1048608 | tf_op jit(solution)/shard_map/while/body/eval_jaxpr/ppermute | solution.py:11
  516.4 58.8 %reduce-scatter.2.cloned.1.call-done = f32[1,128,256]{2,1,0:T(8,128)} async-done(((f32[16,128,256]{2,1,0:T(8,128)}), f32[1,128,256]{2,1,0:T(8,128)}) %reduce-scatter.2.cloned.1.call-update) | async-done | bytes 131088 | tf_op jit(solution)/shard_map/while/body/eval_jaxpr/reduce_scatter | solution.py:41
  577.0 34.8 %all-gather.2.cloned.1.call-done = bf16[16,128,256]{2,1,0:T(8,128)(2,1)} async-done(((bf16[1,128,256]{2,1,0:T(8,128)(2,1)}), bf16[16,128,256]{2,1,0:T(8,128)(2,1)}) %all-gather.2.cloned.1.call-update) | async-done | bytes 1048592 | tf_op jit(solution)/shard_map/while/body/eval_jaxpr/all_gather | solution.py:43
  622.5 25.8 %collective-permute-done = f32[1024,256]{1,0:T(8,128)S(1)} collective-permute-done((f32[1024,256]{1,0:T(8,128)}, f32[1024,256]{1,0:T(8,128)S(1)}, u32[]{:S(2)}, u32[]{:S(2)}) %collective-permute-start) | collective-permute-done | bytes 1048608 | tf_op jit(solution)/shard_map/while/body/eval_jaxpr/ppermute | solution.py:11
  667.1 58.8 %reduce-scatter.2.cloned.1.call-done = f32[1,128,256]{2,1,0:T(8,128)} async-done(((f32[16,128,256]{2,1,0:T(8,128)}), f32[1,128,256]{2,1,0:T(8,128)}) %reduce-scatter.2.cloned.1.call-update) | async-done | bytes 131088 | tf_op jit(solution)/shard_map/while/body/eval_jaxpr/reduce_scatter | solution.py:41
  727.7 34.8 %all-gather.2.cloned.1.call-done = bf16[16,128,256]{2,1,0:T(8,128)(2,1)} async-done(((bf16[1,128,256]{2,1,0:T(8,128)(2,1)}), bf16[16,128,256]{2,1,0:T(8,128)(2,1)}) %all-gather.2.cloned.1.call-update) | async-done | bytes 1048592 | tf_op jit(solution)/shard_map/while/body/eval_jaxpr/all_gather | solution.py:43
  773.3 25.8 %collective-permute-done = f32[1024,256]{1,0:T(8,128)S(1)} collective-permute-done((f32[1024,256]{1,0:T(8,128)}, f32[1024,256]{1,0:T(8,128)S(1)}, u32[]{:S(2)}, u32[]{:S(2)}) %collective-permute-start) | collective-permute-done | bytes 1048608 | tf_op jit(solution)/shard_map/while/body/eval_jaxpr/ppermute | solution.py:11
  817.8 58.8 %reduce-scatter.2.cloned.1.call-done = f32[1,128,256]{2,1,0:T(8,128)} async-done(((f32[16,128,256]{2,1,0:T(8,128)}), f32[1,128,256]{2,1,0:T(8,128)}) %reduce-scatter.2.cloned.1.call-update) | async-done | bytes 131088 | tf_op jit(solution)/shard_map/while/body/eval_jaxpr/reduce_scatter | solution.py:41
  878.4 34.8 %all-gather.2.cloned.1.call-done = bf16[16,128,256]{2,1,0:T(8,128)(2,1)} async-done(((bf16[1,128,256]{2,1,0:T(8,128)(2,1)}), bf16[16,128,256]{2,1,0:T(8,128)(2,1)}) %all-gather.2.cloned.1.call-update) | async-done | bytes 1048592 | tf_op jit(solution)/shard_map/while/body/eval_jaxpr/all_gather | solution.py:43
  968.5 58.9 %reduce-scatter.2.cloned.1.call-done = f32[1,128,256]{2,1,0:T(8,128)} async-done(((f32[16,128,256]{2,1,0:T(8,128)}), f32[1,128,256]{2,1,0:T(8,128)}) %reduce-scatter.2.cloned.1.call-update) | async-done | bytes 131088 | tf_op jit(solution)/shard_map/while/body/eval_jaxpr/reduce_scatter | solution.py:41
  1029.2 34.8 %all-gather.2.cloned.1.call-done = bf16[16,128,256]{2,1,0:T(8,128)(2,1)} async-done(((bf16[1,128,256]{2,1,0:T(8,128)(2,1)}), bf16[16,128,256]{2,1,0:T(8,128)(2,1)}) %all-gather.2.cloned.1.call-update) | async-done | bytes 1048592 | tf_op jit(solution)/shard_map/while/body/eval_jaxpr/all_gather | solution.py:43
  1119.3 58.8 %reduce-scatter.2.cloned.1.call-done = f32[1,128,256]{2,1,0:T(8,128)} async-done(((f32[16,128,256]{2,1,0:T(8,128)}), f32[1,128,256]{2,1,0:T(8,128)}) %reduce-scatter.2.cloned.1.call-update) | async-done | bytes 131088 | tf_op jit(solution)/shard_map/while/body/eval_jaxpr/reduce_scatter | solution.py:41
  1179.9 34.9 %all-gather.2.cloned.1.call-done = bf16[16,128,256]{2,1,0:T(8,128)(2,1)} async-done(((bf16[1,128,256]{2,1,0:T(8,128)(2,1)}), bf16[16,128,256]{2,1,0:T(8,128)(2,1)}) %all-gather.2.cloned.1.call-update) | async-done | bytes 1048592 | tf_op jit(solution)/shard_map/while/body/eval_jaxpr/all_gather | solution.py:43
  1225.6 25.8 %collective-permute-done = f32[1024,256]{1,0:T(8,128)S(1)} collective-permute-done((f32[1024,256]{1,0:T(8,128)}, f32[1024,256]{1,0:T(8,128)S(1)}, u32[]{:S(2)}, u32[]{:S(2)}) %collective-permute-start) | collective-permute-done | bytes 1048608 | tf_op jit(solution)/shard_map/while/body/eval_jaxpr/ppermute | solution.py:11
  (201 shorter events, 307.9 us)
Async XLA Ops:
  41.0 81.9 %reduce-scatter.2.cloned.1.call-start = ((), (), s32[]{:S(2)}) async-start(), calls=%async_computation.1 | async-start | bytes 2228224 | tf_op jit(solution)/shard_map/while/body/eval_jaxpr/reduce_scatter | solution.py:41
  59.7 99.9 %all-gather.2.cloned.1.call-start = ((), (), s32[]{:S(2)}) async-start(), calls=%async_computation.2 | async-start | bytes 1114112 | tf_op jit(solution)/shard_map/while/body/eval_jaxpr/all_gather | solution.py:43
  167.8 28.3 %collective-permute-start = (f32[1024,256]{1,0:T(8,128)}, f32[1024,256]{1,0:T(8,128)S(1)}, u32[]{:S(2)}, u32[]{:S(2)}) collective-permute-start(f32[1024,256]{1,0:T(8,128)} %fusion.27), channel_id=1, source_target_pairs={{0,16},{16,32},{32,48},{48,64},{64,80},{80,96},{96,112},{112,0},{1... | collective-permute-start | bytes 3145736 | tf_op jit(solution)/shard_map/while/body/eval_jaxpr/ppermute | solution.py:11
  196.2 77.7 %reduce-scatter.2.cloned.1.call-start = ((), (), s32[]{:S(2)}) async-start(), calls=%async_computation.1 | async-start | bytes 2228224 | tf_op jit(solution)/shard_map/while/body/eval_jaxpr/reduce_scatter | solution.py:41
  214.8 95.5 %all-gather.2.cloned.1.call-start = ((), (), s32[]{:S(2)}) async-start(), calls=%async_computation.2 | async-start | bytes 1114112 | tf_op jit(solution)/shard_map/while/body/eval_jaxpr/all_gather | solution.py:43
  318.6 28.3 %collective-permute-start = (f32[1024,256]{1,0:T(8,128)}, f32[1024,256]{1,0:T(8,128)S(1)}, u32[]{:S(2)}, u32[]{:S(2)}) collective-permute-start(f32[1024,256]{1,0:T(8,128)} %fusion.27), channel_id=1, source_target_pairs={{0,16},{16,32},{32,48},{48,64},{64,80},{80,96},{96,112},{112,0},{1... | collective-permute-start | bytes 3145736 | tf_op jit(solution)/shard_map/while/body/eval_jaxpr/ppermute | solution.py:11
  346.9 77.6 %reduce-scatter.2.cloned.1.call-start = ((), (), s32[]{:S(2)}) async-start(), calls=%async_computation.1 | async-start | bytes 2228224 | tf_op jit(solution)/shard_map/while/body/eval_jaxpr/reduce_scatter | solution.py:41
  365.6 95.5 %all-gather.2.cloned.1.call-start = ((), (), s32[]{:S(2)}) async-start(), calls=%async_computation.2 | async-start | bytes 1114112 | tf_op jit(solution)/shard_map/while/body/eval_jaxpr/all_gather | solution.py:43
  469.4 28.3 %collective-permute-start = (f32[1024,256]{1,0:T(8,128)}, f32[1024,256]{1,0:T(8,128)S(1)}, u32[]{:S(2)}, u32[]{:S(2)}) collective-permute-start(f32[1024,256]{1,0:T(8,128)} %fusion.27), channel_id=1, source_target_pairs={{0,16},{16,32},{32,48},{48,64},{64,80},{80,96},{96,112},{112,0},{1... | collective-permute-start | bytes 3145736 | tf_op jit(solution)/shard_map/while/body/eval_jaxpr/ppermute | solution.py:11
  497.7 77.5 %reduce-scatter.2.cloned.1.call-start = ((), (), s32[]{:S(2)}) async-start(), calls=%async_computation.1 | async-start | bytes 2228224 | tf_op jit(solution)/shard_map/while/body/eval_jaxpr/reduce_scatter | solution.py:41
  516.3 95.4 %all-gather.2.cloned.1.call-start = ((), (), s32[]{:S(2)}) async-start(), calls=%async_computation.2 | async-start | bytes 1114112 | tf_op jit(solution)/shard_map/while/body/eval_jaxpr/all_gather | solution.py:43
  620.0 28.3 %collective-permute-start = (f32[1024,256]{1,0:T(8,128)}, f32[1024,256]{1,0:T(8,128)S(1)}, u32[]{:S(2)}, u32[]{:S(2)}) collective-permute-start(f32[1024,256]{1,0:T(8,128)} %fusion.27), channel_id=1, source_target_pairs={{0,16},{16,32},{32,48},{48,64},{64,80},{80,96},{96,112},{112,0},{1... | collective-permute-start | bytes 3145736 | tf_op jit(solution)/shard_map/while/body/eval_jaxpr/ppermute | solution.py:11
  648.4 77.6 %reduce-scatter.2.cloned.1.call-start = ((), (), s32[]{:S(2)}) async-start(), calls=%async_computation.1 | async-start | bytes 2228224 | tf_op jit(solution)/shard_map/while/body/eval_jaxpr/reduce_scatter | solution.py:41
  667.0 95.5 %all-gather.2.cloned.1.call-start = ((), (), s32[]{:S(2)}) async-start(), calls=%async_computation.2 | async-start | bytes 1114112 | tf_op jit(solution)/shard_map/while/body/eval_jaxpr/all_gather | solution.py:43
  770.8 28.3 %collective-permute-start = (f32[1024,256]{1,0:T(8,128)}, f32[1024,256]{1,0:T(8,128)S(1)}, u32[]{:S(2)}, u32[]{:S(2)}) collective-permute-start(f32[1024,256]{1,0:T(8,128)} %fusion.27), channel_id=1, source_target_pairs={{0,16},{16,32},{32,48},{48,64},{64,80},{80,96},{96,112},{112,0},{1... | collective-permute-start | bytes 3145736 | tf_op jit(solution)/shard_map/while/body/eval_jaxpr/ppermute | solution.py:11
  799.1 77.5 %reduce-scatter.2.cloned.1.call-start = ((), (), s32[]{:S(2)}) async-start(), calls=%async_computation.1 | async-start | bytes 2228224 | tf_op jit(solution)/shard_map/while/body/eval_jaxpr/reduce_scatter | solution.py:41
  817.8 95.5 %all-gather.2.cloned.1.call-start = ((), (), s32[]{:S(2)}) async-start(), calls=%async_computation.2 | async-start | bytes 1114112 | tf_op jit(solution)/shard_map/while/body/eval_jaxpr/all_gather | solution.py:43
  921.5 28.3 %collective-permute-start = (f32[1024,256]{1,0:T(8,128)}, f32[1024,256]{1,0:T(8,128)S(1)}, u32[]{:S(2)}, u32[]{:S(2)}) collective-permute-start(f32[1024,256]{1,0:T(8,128)} %fusion.27), channel_id=1, source_target_pairs={{0,16},{16,32},{32,48},{48,64},{64,80},{80,96},{96,112},{112,0},{1... | collective-permute-start | bytes 3145736 | tf_op jit(solution)/shard_map/while/body/eval_jaxpr/ppermute | solution.py:11
  949.8 77.6 %reduce-scatter.2.cloned.1.call-start = ((), (), s32[]{:S(2)}) async-start(), calls=%async_computation.1 | async-start | bytes 2228224 | tf_op jit(solution)/shard_map/while/body/eval_jaxpr/reduce_scatter | solution.py:41
  968.4 95.6 %all-gather.2.cloned.1.call-start = ((), (), s32[]{:S(2)}) async-start(), calls=%async_computation.2 | async-start | bytes 1114112 | tf_op jit(solution)/shard_map/while/body/eval_jaxpr/all_gather | solution.py:43
  1072.3 28.3 %collective-permute-start = (f32[1024,256]{1,0:T(8,128)}, f32[1024,256]{1,0:T(8,128)S(1)}, u32[]{:S(2)}, u32[]{:S(2)}) collective-permute-start(f32[1024,256]{1,0:T(8,128)} %fusion.27), channel_id=1, source_target_pairs={{0,16},{16,32},{32,48},{48,64},{64,80},{80,96},{96,112},{112,0},{1... | collective-permute-start | bytes 3145736 | tf_op jit(solution)/shard_map/while/body/eval_jaxpr/ppermute | solution.py:11
  1100.6 77.5 %reduce-scatter.2.cloned.1.call-start = ((), (), s32[]{:S(2)}) async-start(), calls=%async_computation.1 | async-start | bytes 2228224 | tf_op jit(solution)/shard_map/while/body/eval_jaxpr/reduce_scatter | solution.py:41
  1119.2 95.6 %all-gather.2.cloned.1.call-start = ((), (), s32[]{:S(2)}) async-start(), calls=%async_computation.2 | async-start | bytes 1114112 | tf_op jit(solution)/shard_map/while/body/eval_jaxpr/all_gather | solution.py:43
  1223.1 28.3 %collective-permute-start = (f32[1024,256]{1,0:T(8,128)}, f32[1024,256]{1,0:T(8,128)S(1)}, u32[]{:S(2)}, u32[]{:S(2)}) collective-permute-start(f32[1024,256]{1,0:T(8,128)} %fusion.27), channel_id=1, source_target_pairs={{0,16},{16,32},{32,48},{48,64},{64,80},{80,96},{96,112},{112,0},{1... | collective-permute-start | bytes 3145736 | tf_op jit(solution)/shard_map/while/body/eval_jaxpr/ppermute | solution.py:11
  (27 other events, 429.1 us)
Sparse Core Ops, SparseCore 0:
  59.8 63.0 reduce-scatter.1
  124.8 34.7 all-gather.1
  214.9 58.8 reduce-scatter.1
  275.7 34.6 all-gather.1
  365.7 58.7 reduce-scatter.1
  426.3 34.7 all-gather.1
  516.5 58.6 reduce-scatter.1
  577.0 34.7 all-gather.1
  667.1 58.7 reduce-scatter.1
  727.8 34.7 all-gather.1
  817.9 58.6 reduce-scatter.1
  878.4 34.7 all-gather.1
  968.6 58.7 reduce-scatter.1
  1029.2 34.7 all-gather.1
  1119.3 58.6 reduce-scatter.1
  1179.9 34.8 all-gather.1
where the time goes:
time: 1260 us
  waiting for transfers between devices  960 us (76%)
  other arithmetic  125 us (10%)
  matrix products  60.8 us (5%)
  local copies, waits for them, and re-layouts  50.2 us (4%)
  blocking collectives  28.5 us (2%)
  starting transfers between devices  20.2 us (2%)
  between operations  13.1 us (1%)
    reduce_scatter x8, waiting for transfers between devices, update(): lax.psum_scatter(partial_sums, 'tile', scatter_dimension=0, tiled=True)  475 us
    all_gather x8, waiting for transfers between devices, update(): residual_all = lax.all_gather(residual, 'tile', axis=0, tiled=True)  278 us
    ppermute x8, waiting for transfers between devices, passed_along(): lax.ppermute(value, axis, [(i, (i + by) % devices) for i in range(devices)])  207 us
    scatter-add x8, other arithmetic, update(): partial_sums = jnp.zeros((ray_blocks, block, width), jnp.float32).at[flat...  99.8 us
    dot_general x8, matrix products, update(): jnp.einsum('qkrp,qps->qkrs', tile_set, image, preferred_element_type=jnp....  36.2 us
    gather x8, local copies, waits for them, and re-layouts, update(): chosen = residual_all[links]  31.7 us
    unnamed x1, blocking collectives  28.5 us
  transfers between devices with their start and end apart: 24, of which 24 were waited for; matrix products, arithmetic and copies ran while one was open for 0% of the time, Pallas kernels for 0%

commit v1 on v0

v1 whole, which is shorter than its diff:
```python
import jax
import jax.numpy as jnp
from jax import lax
from jax.experimental import pallas as pl
from jax.experimental.pallas import tpu as pltpu
from jax.sharding import PartitionSpec as P

MESH = pl.DeviceIdType.MESH
BLK = 128
STEPS = 8
CHIPS = 8
COLS = 256
PAD = 16
ROWS = COLS + PAD
PIXELS = 1024
RAYS = 2048
CHUNKS = ((0, 144), (144, 128))


def split3(w):
    row = lax.broadcasted_iota(jnp.int32, w.shape, 0)
    hi = w.astype(jnp.bfloat16).astype(jnp.float32)
    rest = w - hi
    mid = rest.astype(jnp.bfloat16).astype(jnp.float32)
    low = rest - mid
    out = jnp.where(row == 0, hi, jnp.where(row == 1, mid, jnp.where(row == 2, low, 0.0)))
    return out.astype(jnp.bfloat16)


def kernel(
    vol_ref, tile_ref, inv_ref, inv0_ref, proj_ref, out_ref,
    tb, inv_v, inv_s, pm, dense, xe, mine, c1s, c1r, rss, rs, loc, wtot, re,
    tile_sem, inv_send, inv_recv, inv_copy, pm_send, pm_recv, t_send, t_recv,
    c1_send, c1_recv, rs_send, rs_recv, ag_send, ag_recv, c2_send, c2_recv,
):
    c = lax.axis_index("subset")
    t = lax.axis_index("tile")
    z, h = c // 2, c % 2
    x, l, k = t // 4, (t // 2) % 2, t % 2

    def chip(mr):
        return (c, (((x + mr // 2) % 4) * 2 + (l + mr % 2) % 2) * 2 + k)

    def back(mr):
        return ((4 - mr // 2) % 4) * 2 + mr % 2

    core = (c, t + 1 - 2 * k)

    def group(d):
        return ((c + d) % STEPS, t)

    z_dev = {-1: (((z + 3) % 4) * 2 + h, t), 1: (((z + 1) % 4) * 2 + h, t)}
    y_dev = (z * 2 + 1 - h, t)

    own = pltpu.make_async_copy(tile_ref, tb[0], tile_sem)
    own.start()

    barrier = pltpu.get_barrier_semaphore()
    for mr in range(1, CHIPS):
        pl.semaphore_signal(barrier, inc=1, device_id=chip(mr), device_id_type=MESH)
    pl.semaphore_signal(barrier, inc=1, device_id=core, device_id_type=MESH)
    for d in range(1, STEPS):
        pl.semaphore_signal(barrier, inc=1, device_id=group(d), device_id_type=MESH)
    pl.semaphore_wait(barrier, CHIPS - 1 + 1 + STEPS - 1)
    own.wait()

    def piece(slot, p):
        return tb[slot].at[pl.ds(4 * p, 4)]

    def tile_copy(idx, src, p, dst, device):
        return pltpu.make_async_remote_copy(
            src_ref=piece(src, p), dst_ref=piece(dst, p), send_sem=t_send.at[idx],
            recv_sem=t_recv.at[dst, p], device_id=device, device_id_type=MESH,
        )

    flows = (
        {
            0: [("-", 0, 0, 2), ("+", 0, 0, 6), ("y", 0, 1, 7)],
            1: [("-", 1, 1, 3), ("+", 6, 0, 4), ("y", 2, 0, 1)],
            2: [("-", 0, 1, 2), ("+", 0, 1, 6), ("y", 4, 0, 3)],
            3: [("-", 3, 1, 5), ("+", 1, 1, 7), ("y", 6, 0, 5)],
            4: [("-", 2, 1, 4), ("y", 0, 0, 7)],
        },
        {
            0: [("-", 0, 0, 2), ("+", 0, 0, 6), ("y", 0, 1, 1)],
            1: [("-", 7, 1, 1), ("+", 6, 0, 4), ("y", 0, 0, 1)],
            2: [("-", 0, 1, 2), ("+", 0, 1, 6), ("y", 2, 0, 3)],
            3: [("-", 1, 1, 3), ("+", 7, 1, 5), ("y", 4, 0, 5)],
            4: [("-", 2, 1, 4), ("y", 6, 0, 7)],
        },
    )
    waited = (set(), set())

    def need(row, slot, p):
        if slot and (slot, p) not in waited[row]:
            waited[row].add((slot, p))
            pltpu.make_async_remote_copy(
                src_ref=piece(slot, p), dst_ref=piece(slot, p), send_sem=t_send.at[0],
                recv_sem=t_recv.at[slot, p], device_id=y_dev, device_id_type=MESH,
            ).wait_recv()

    def flow_copies(row, point):
        for i, (way, src, p, dst) in enumerate(flows[row][point]):
            device = y_dev if way == "y" else z_dev[-1 if way == "-" else 1]
            yield src, p, tile_copy(3 * point + i, src, p, dst, device)

    def tile_point(point):
        for row in range(2):
            @pl.when(h == row)
            def _():
                for src, p, copy in flow_copies(row, point):
                    need(row, src, p)
                    copy.start()

    def tile_drain():
        for row in range(2):
            @pl.when(h == row)
            def _():
                for point in range(5):
                    for _, _, copy in flow_copies(row, point):
                        copy.wait_send()

    def tile_wait(slot):
        for row in range(2):
            @pl.when(h == row)
            def _():
                need(row, slot, 0)
                need(row, slot, 1)

    def pm_copy(slot):
        d = STEPS - slot
        return pltpu.make_async_remote_copy(
            src_ref=proj_ref.at[pl.ds(pl.multiple_of(((c + d) % STEPS) * COLS, COLS), COLS)],
            dst_ref=pm.at[slot], send_sem=pm_send.at[slot], recv_sem=pm_recv.at[slot],
            device_id=group(d), device_id_type=MESH,
        )

    def inv_copy_to(slot):
        return pltpu.make_async_remote_copy(
            src_ref=inv_ref, dst_ref=inv_v.at[slot], send_sem=inv_send.at[slot],
            recv_sem=inv_recv.at[slot], device_id=group(STEPS - slot), device_id_type=MESH,
        )

    for slot in range(1, STEPS):
        inv_copy_to(slot).start()
    pm_copy(1).start()
    tile_point(0)

    def assemble(slot):
        dn = dense.at[slot % 2]
        if slot:
            inv_copy_to(slot).wait_recv()
            local = pltpu.make_async_copy(inv_v.at[slot], inv_s.at[slot], inv_copy)
            local.start()
            local.wait()
            tile_wait(slot)

        def block(i, _):
            mr, j = i // 2, i % 2
            b = (((x + mr // 2) % 4) * 2 + (l + mr % 2) % 2) * 2 + (k + j) % 2
            for q in range(8):
                at = inv_s[slot, q, b] if slot else inv0_ref[q, b]
                tile = tb[slot][q, jnp.minimum(at, 7)]
                dn[pl.ds(pl.multiple_of(i * BLK, BLK), BLK), q * BLK:(q + 1) * BLK] = jnp.where(
                    at < 8, tile, jnp.zeros_like(tile)
                )
            return 0

        lax.fori_loop(0, 16, block, 0)

    def c1_copy(mr):
        return pltpu.make_async_remote_copy(
            src_ref=c1s.at[mr], dst_ref=c1r.at[mr], send_sem=c1_send.at[mr],
            recv_sem=c1_recv.at[mr], device_id=core, device_id_type=MESH,
        )

    def rs_copy(mr, ch):
        at, n = CHUNKS[ch]
        return pltpu.make_async_remote_copy(
            src_ref=rss.at[mr, pl.ds(at, n)], dst_ref=rs.at[back(mr), pl.ds(at, n)],
            send_sem=rs_send.at[ch, mr], recv_sem=rs_recv.at[ch, back(mr)],
            device_id=chip(mr), device_id_type=MESH,
        )

    def ag_copy(mr, ch):
        rows = pl.ds(PAD + 128 * ch, 128)
        return pltpu.make_async_remote_copy(
            src_ref=re.at[0, 0, rows], dst_ref=re.at[0, back(mr), rows],
            send_sem=ag_send.at[ch, mr], recv_sem=ag_recv.at[ch, back(mr)],
            device_id=chip(mr), device_id_type=MESH,
        )

    def c2_copy(ch):
        rows = pl.ds(PAD + 128 * ch, 128)
        return pltpu.make_async_remote_copy(
            src_ref=re.at[0, :, rows], dst_ref=re.at[1, :, rows], send_sem=c2_send.at[ch],
            recv_sem=c2_recv.at[ch], device_id=core, device_id_type=MESH,
        )

    def each(first, last, body):
        def step(i, _):
            body(i)
            return 0

        lax.fori_loop(first, last, step, 0)

    out_ref[...] = vol_ref[...]
    xe[0:PAD] = jnp.ones((PAD, PIXELS), jnp.bfloat16)
    xe[PAD:] = vol_ref[...].astype(jnp.bfloat16)
    re[:, :, 0:PAD] = jnp.ones((2, CHIPS, PAD, BLK), jnp.bfloat16)
    assemble(0)

    for step in range(STEPS):
        dn = dense.at[step % 2]

        def forward(i):
            mr = CHIPS - 1 - i
            rows = dn[pl.ds(pl.multiple_of(mr * 256, 256), 256), :]
            y = lax.dot_general(
                xe[...], rows, (((1,), (1,)), ((), ())), preferred_element_type=jnp.float32
            )
            w = y[0:PAD]
            diff = y[PAD:] - y[0:1]
            mine[mr, 0:PAD] = w[:, :BLK]
            mine[mr, PAD:] = diff[:, :BLK]
            c1s[mr, 0:PAD] = split3(w[:, BLK:])
            c1s[mr, PAD:] = diff[:, BLK:].astype(jnp.bfloat16)
            c1_copy(mr).start()

        each(0, CHIPS, forward)
        if step + 2 < STEPS:
            pm_copy(step + 2).start()

        def chip_sum0(i):
            mr = CHIPS - 1 - i
            c1_copy(mr).wait_recv()
            w = mine[mr, 0:PAD] + jnp.sum(c1r[mr, 0:PAD].astype(jnp.float32), axis=0, keepdims=True)
            rss[mr, 0:PAD] = split3(w)
            n = CHUNKS[0][1]
            rss[mr, PAD:n] = (mine[mr, PAD:n] + c1r[mr, PAD:n].astype(jnp.float32)).astype(jnp.bfloat16)
            rs_copy(mr, 0).start()

        def chip_sum1(i):
            mr = CHIPS - 1 - i
            at = CHUNKS[1][0]
            rss[mr, at:] = (mine[mr, at:] + c1r[mr, at:].astype(jnp.float32)).astype(jnp.bfloat16)
            rs_copy(mr, 1).start()

        each(0, CHIPS - 1, chip_sum0)
        each(0, CHIPS - 1, chip_sum1)
        c1_copy(0).wait_recv()
        loc[0:PAD] = mine[0, 0:PAD] + jnp.sum(c1r[0, 0:PAD].astype(jnp.float32), axis=0, keepdims=True)
        loc[PAD:] = mine[0, PAD:] + c1r[0, PAD:].astype(jnp.float32)
        if step:
            pm_copy(step).wait_recv()

        for ch in range(2):
            each(1, CHIPS, lambda mr: rs_copy(mr, ch).wait_recv())
            at, n = CHUNKS[ch]
            if ch == 0:
                weights = rs[1, 0:PAD].astype(jnp.float32)
                for mr in range(2, CHIPS):
                    weights += rs[mr, 0:PAD].astype(jnp.float32)
                wtot[...] = loc[0:PAD] + jnp.sum(weights, axis=0, keepdims=True)
            first = max(at, PAD)
            total = loc[first:at + n]
            for mr in range(1, CHIPS):
                total += rs[mr, first:at + n].astype(jnp.float32)
            if step:
                measured = pm[step, 128 * ch:128 * ch + 128]
            else:
                measured = proj_ref[pl.ds(pl.multiple_of(c * COLS + 128 * ch, 128), 128), :]
            re[0, 0, first:at + n] = ((measured - 1.0) - total / wtot[0:1]).astype(jnp.bfloat16)
            each(1, CHIPS, lambda i: ag_copy(CHIPS - i, ch).start())

        for ch in range(2):
            each(1, CHIPS, lambda mr: ag_copy(mr, ch).wait_recv())
            c2_copy(ch).start()
        each(0, CHIPS, lambda mr: c1_copy(mr).wait_send())
        for ch in range(2):
            each(1, CHIPS, lambda mr: rs_copy(mr, ch).wait_send())
            each(1, CHIPS, lambda mr: ag_copy(mr, ch).wait_send())
        for ch in range(2):
            c2_copy(ch).wait()

        def backward(n):
            cols = pl.ds(pl.multiple_of(n * 256, 256), 256)
            acc = jnp.zeros((ROWS, 256), jnp.float32)
            for mr in range(CHIPS):
                lhs = jnp.concatenate([re[0, mr], re[1, mr]], axis=1)
                acc += jnp.dot(
                    lhs, dn[mr * 256:(mr + 1) * 256, cols], preferred_element_type=jnp.float32
                )
            new = out_ref[:, cols] + 0.9 * acc[PAD:] / acc[0:1]
            out_ref[:, cols] = new
            xe[PAD:, cols] = new.astype(jnp.bfloat16)

        each(0, 4, backward)
        if step == 0:
            tile_point(1)
        if step == 1:
            tile_point(3)
        if step == 2:
            tile_point(4)
        if step + 1 < STEPS:
            assemble(step + 1)
        if step == 0:
            tile_point(2)

    tile_drain()
    for slot in range(1, STEPS):
        inv_copy_to(slot).wait_send()
        pm_copy(slot).wait_send()


def per_device(start_volume, tiles, pattern, projections):
    entry = jnp.arange(8, dtype=jnp.int32)[None, :, None]
    name = jnp.arange(BLK, dtype=jnp.int32)[None, None, :]
    inverse = jnp.min(jnp.where(pattern[0][:, :, None] == name, entry, 8), axis=1)
    vmem = pl.BlockSpec(memory_space=pltpu.VMEM)
    bf16, f32, i32 = jnp.bfloat16, jnp.float32, jnp.int32
    dma = pltpu.SemaphoreType.DMA
    out = pl.pallas_call(
        kernel,
        out_shape=jax.ShapeDtypeStruct((COLS, PIXELS), f32),
        in_specs=[
            vmem, pl.BlockSpec(memory_space=pl.ANY), vmem,
            pl.BlockSpec(memory_space=pltpu.SMEM), vmem,
        ],
        out_specs=vmem,
        scratch_shapes=[
            [pltpu.VMEM((8, 8, BLK, BLK), bf16)] * STEPS,
            pltpu.VMEM((STEPS, 8, BLK), i32),
            pltpu.SMEM((STEPS, 8, BLK), i32),
            pltpu.VMEM((STEPS, COLS, BLK), f32),
            pltpu.VMEM((2, RAYS, PIXELS), bf16),
            pltpu.VMEM((ROWS, PIXELS), bf16),
            pltpu.VMEM((CHIPS, ROWS, BLK), f32),
            pltpu.VMEM((CHIPS, ROWS, BLK), bf16),
            pltpu.VMEM((CHIPS, ROWS, BLK), bf16),
            pltpu.VMEM((CHIPS, ROWS, BLK), bf16),
            pltpu.VMEM((CHIPS, ROWS, BLK), bf16),
            pltpu.VMEM((ROWS, BLK), f32),
            pltpu.VMEM((PAD, BLK), f32),
            pltpu.VMEM((2, CHIPS, ROWS, BLK), bf16),
            dma, dma((STEPS,)), dma((STEPS,)), dma, dma((STEPS,)), dma((STEPS,)),
            dma((15,)), dma((STEPS, 2)),
            dma((CHIPS,)), dma((CHIPS,)), dma((2, CHIPS)), dma((2, CHIPS)),
            dma((2, CHIPS)), dma((2, CHIPS)), dma((2,)), dma((2,)),
        ],
        compiler_params=pltpu.CompilerParams(
            collective_id=0, has_side_effects=True, vmem_limit_bytes=56 * 2**20
        ),
        cost_estimate=pl.CostEstimate(
            flops=STEPS * 4 * RAYS * PIXELS * COLS, bytes_accessed=6 * 2**20, transcendentals=0
        ),
        name="sweep",
    )(start_volume.T, tiles[0], inverse, inverse, projections[0].T)
    return out.T


def solution(mesh):
    in_specs = (
        P("tile", "subset"),
        P("subset", "tile", None, None, None),
        P("subset", "tile", None),
        P("subset", "tile", None),
    )
    return jax.shard_map(
        per_device, mesh=mesh, in_specs=in_specs, out_specs=P("tile", "subset"), check_vma=False
    )
```

time: 1260 us -> 317 us (0.25)
  waiting for transfers between devices: 960 us -> 0 us
  Pallas kernels: 0 us -> 309 us
  other arithmetic: 125 us -> 1.46 us
  matrix products: 60.8 us -> 0 us
  local copies, waits for them, and re-layouts: 50.2 us -> 6.39 us
  blocking collectives: 28.5 us -> 0 us
  starting transfers between devices: 20.2 us -> 0 us
  between operations: 13.1 us -> 0.01 us
    reduce_scatter x8 -> x0, waiting for transfers between devices: 475 us -> none  [update(): lax.psum_scatter(partial_sums, 'tile', scatter_dimension=0, tiled=True)]
    pallas_call x0 -> x1, Pallas kernels: none -> 309 us  [per_device(): pl.pallas_call(kernel, out_shape=jax.ShapeDtypeStruct((COLS, PIXELS), f32...]
    all_gather x8 -> x0, waiting for transfers between devices: 278 us -> none  [update(): residual_all = lax.all_gather(residual, 'tile', axis=0, tiled=True)]
    ppermute x8 -> x0, waiting for transfers between devices: 207 us -> none  [passed_along(): lax.ppermute(value, axis, [(i, (i + by) % devices) for i in range(devices)])]
    scatter-add x9 -> x0, other arithmetic: 101 us -> none  [the longest x8 99.8 us: update(): partial_sums = jnp.zeros((ray_blocks, block, width), jnp.float32).at[flat...]
    dot_general x16 -> x0, matrix products: 60.8 us -> none  [the longest x8 36.2 us: update(): jnp.einsum('qkrp,qps->qkrs', tile_set, image, preferred_element_type=jnp....]
    gather x8 -> x0, local copies, waits for them, and re-layouts: 31.7 us -> none  [update(): chosen = residual_all[links]]
    unnamed x1 -> x0, blocking collectives: 28.5 us -> none
  transfers between devices with their start and end apart: 24 -> 0, of which waited for: 24 -> 0; matrix products, arithmetic and copies ran while one was open for 0% -> 0% of each run, Pallas kernels for 0% -> 0%
where the time goes in v1:
time: 317 us
  Pallas kernels  309 us (97%)
  local copies, waits for them, and re-layouts  6.39 us (2%)
    pallas_call x1, Pallas kernels, per_device(): pl.pallas_call(kernel, out_shape=jax.ShapeDtypeStruct((COLS, PIXELS), f32...  309 us

profile of v1, /device:TPU:1, one launch (start us, length us, event | category | flops | bytes accessed | tf_op | source)
XLA Modules:
  0.0 317.1 jit_solution(5272933956968576344)
XLA Ops:
  0.0 0.0 copy-start
  0.0 1.5 select_reduce_fusion.inv_ref.inv0_ref
  1.5 2.5 copy.8
  4.0 0.0 copy-done
  4.0 1.3 copy.9
  5.3 309.3 %sweep.1 = f32[256,1024]{1,0:T(8,128)} custom-call(f32[256,1024]{1,0:T(8,128)} %bitcast.8, bf16[8,8,128,128]{3,2,1,0:T(8,128)(2,1)} %bitcast.11, s32[8,128]{1,0:T(8,128)} %select_reduce_fusion.inv_ref.inv0_ref, s32[8,128]{1,0:T(8,128)} %select_reduce_fusion.inv_ref.inv0_ref, f32[2048,128]{1,0:T(8,128)} %bitcast.9), custom_call_target="tpu_custom_call" | custom-call | flops 17179869184 | bytes 6291456 | tf_op jit(solution)/shard_map/sweep/pallas_call | solution.py:323
  314.6 2.5 copy.10
Async XLA Ops:
  0.0 4.0 %copy-start = (f32[1,128,2048]{2,1,0:T(8,128)S(1)}, f32[1,128,2048]{2,1,0:T(8,128)}, u32[]{:S(2)}) copy-start(f32[1,128,2048]{2,1,0:T(8,128)} %param.7) | copy-start | bytes 3145732

commit v2 on v0

v2 whole, which is shorter than its diff:
```python
import jax
import jax.numpy as jnp
from jax import lax
from jax.experimental import pallas as pl
from jax.experimental.pallas import tpu as pltpu
from jax.sharding import PartitionSpec as P

MESH = pl.DeviceIdType.MESH
BLK = 128
STEPS = 8
CHIPS = 8
EARLY = 6
COLS = 256
PAD = 16
ROWS = COLS + PAD
PIXELS = 1024
RAYS = 2048
HALF = COLS // 2
LEAD = (PAD, 0)
SIZE = (PAD + HALF, HALF)


def split3(w):
    row = lax.broadcasted_iota(jnp.int32, w.shape, 0)
    hi = w.astype(jnp.bfloat16).astype(jnp.float32)
    rest = w - hi
    mid = rest.astype(jnp.bfloat16).astype(jnp.float32)
    low = rest - mid
    out = jnp.where(row == 0, hi, jnp.where(row == 1, mid, jnp.where(row == 2, low, 0.0)))
    return out.astype(jnp.bfloat16)


def kernel(
    vol_ref, tile_ref, inv_ref, inv0_ref, proj_ref, out_ref,
    tb, inv_v, inv_s, pm, dense, xe, wray, wtot, wpix, mine, c1s, c1r, rss, rsx, loc, re,
    tile_sem, inv_send, inv_recv, inv_copy, pm_send, pm_recv, t_send, t_recv,
    c1_send, c1_recv, rs_send, rs_recv, ag_send, ag_recv, c2_send, c2_recv,
):
    c = lax.axis_index("subset")
    t = lax.axis_index("tile")
    z, h = c // 2, c % 2
    x, l, k = t // 4, (t // 2) % 2, t % 2

    def chip(dx, dl):
        return (c, (((x + dx) % 4) * 2 + (l + dl) % 2) * 2 + k)

    core = (c, t + 1 - 2 * k)

    def group(d):
        return ((c + d) % STEPS, t)

    z_dev = {-1: (((z + 3) % 4) * 2 + h, t), 1: (((z + 1) % 4) * 2 + h, t)}
    y_dev = (z * 2 + 1 - h, t)

    def remote(src, dst, send, recv, device):
        return pltpu.make_async_remote_copy(
            src_ref=src, dst_ref=dst, send_sem=send, recv_sem=recv, device_id=device,
            device_id_type=MESH,
        )

    FAR = ((2, 1), (2, 0), (1, 1), (3, 1), (1, 0), (3, 0), (0, 1))

    own = pltpu.make_async_copy(tile_ref, tb[0], tile_sem)
    own.start()

    barrier = pltpu.get_barrier_semaphore()
    partners = [chip(dx, dl) for dx, dl in FAR] + [core]
    partners += [group(d) for d in range(1, STEPS)]
    for device in partners:
        pl.semaphore_signal(barrier, inc=1, device_id=device, device_id_type=MESH)
    pl.semaphore_wait(barrier, len(partners))
    own.wait()

    def piece(slot, p):
        return tb[slot].at[pl.ds(4 * p, 4)]

    def tile_copy(idx, src, p, dst, device):
        return remote(piece(src, p), piece(dst, p), t_send.at[idx], t_recv.at[dst, p], device)

    flows = (
        (
            (("-", 0, 0, 2), ("+", 0, 0, 6), ("y", 0, 1, 7)),
            (("-", 0, 1, 2), ("+", 6, 0, 4), ("y", 2, 0, 1)),
            (("-", 1, 1, 3), ("+", 0, 1, 6), ("y", 0, 0, 7)),
            (("-", 1, 0, 3), ("+", 1, 0, 7)),
            (("-", 2, 1, 4), ("+", 7, 0, 5)),
            (("-", 3, 1, 5), ("+", 1, 1, 7)),
        ),
        (
            (("-", 0, 0, 2), ("+", 0, 0, 6), ("y", 0, 1, 1)),
            (("-", 7, 1, 1), ("+", 7, 1, 5), ("y", 0, 0, 1)),
            (("-", 0, 1, 2), ("+", 5, 1, 3)),
            (("-", 1, 0, 3), ("+", 0, 1, 6)),
            (("-", 2, 0, 4), ("+", 6, 1, 4)),
            (("+", 7, 0, 5),),
        ),
    )
    events = [("send", 0), ("send", 1), ("make", 1), ("send", 2)]
    for slot in range(2, STEPS):
        if slot + 1 < len(flows[0]):
            events.append(("send", slot + 1))
        events.append(("make", slot))
    waits = ({}, {})
    for row in range(2):
        seen = set()
        for kind, at in events:
            if kind == "send":
                reads = sorted({(src, p) for _, src, p, _ in flows[row][at] if src})
            else:
                reads = [(at, 0), (at, 1)]
            waits[row][kind, at] = [r for r in reads if r not in seen]
            seen.update(reads)

    def tile_arrived(row, kind, at):
        for slot, p in waits[row][kind, at]:
            tile_copy(0, slot, p, slot, y_dev).wait_recv()

    def flow_copies(row, point):
        for i, (way, src, p, dst) in enumerate(flows[row][point]):
            device = y_dev if way == "y" else z_dev[-1 if way == "-" else 1]
            yield tile_copy(3 * point + i, src, p, dst, device)

    def tile_point(point):
        for row in range(2):
            @pl.when(h == row)
            def _():
                tile_arrived(row, "send", point)
                for copy in flow_copies(row, point):
                    copy.start()

    def tile_drain():
        for row in range(2):
            @pl.when(h == row)
            def _():
                for point in range(len(flows[row])):
                    for copy in flow_copies(row, point):
                        copy.wait_send()

    def tile_wait(slot):
        for row in range(2):
            @pl.when(h == row)
            def _():
                tile_arrived(row, "make", slot)

    def proj_rows(d):
        return pl.ds(pl.multiple_of(((c + d) % STEPS) * COLS, COLS), COLS)

    def pm_copy(slot):
        d = STEPS - slot
        return remote(
            proj_ref.at[proj_rows(d)], pm.at[slot], pm_send.at[slot], pm_recv.at[slot], group(d)
        )

    def inv_copy_to(slot):
        return remote(
            inv_ref, inv_v.at[slot], inv_send.at[slot], inv_recv.at[slot], group(STEPS - slot)
        )

    for slot in range(1, STEPS):
        inv_copy_to(slot).start()
    pm_copy(1).start()
    tile_point(0)

    def assemble(slot):
        dn = dense.at[slot % 3]
        if slot:
            inv_copy_to(slot).wait_recv()
            local = pltpu.make_async_copy(inv_v.at[slot], inv_s.at[slot], inv_copy)
            local.start()
            local.wait()
            tile_wait(slot)

        def block(i, _):
            mr, j = i // 2, i % 2
            b = (((x + mr % 4) % 4) * 2 + (l + mr // 4) % 2) * 2 + (k + j) % 2
            for q in range(8):
                at = inv_s[slot, q, b] if slot else inv0_ref[q, b]
                tile = tb[slot][q, jnp.minimum(at, 7)]
                dn[pl.ds(pl.multiple_of(i * BLK, BLK), BLK), q * BLK:(q + 1) * BLK] = jnp.where(
                    at < 8, tile, jnp.zeros_like(tile)
                )
            return 0

        lax.fori_loop(0, 16, block, 0)

    def c1_copy(hf, dl):
        part = pl.ds(4 * dl, 4)
        return remote(
            c1s[hf].at[part], c1r[hf].at[part], c1_send.at[hf, dl], c1_recv.at[hf, dl], core
        )

    def rs_copy(hf, dx, dl):
        out, into = 4 * dl + dx, 4 * dl + (4 - dx) % 4
        return remote(
            rss[hf].at[out], rsx[hf].at[into], rs_send.at[hf, out], rs_recv.at[hf, into],
            chip(dx, dl),
        )

    def ag_copy(hf, dx, dl):
        rows = pl.ds(LEAD[hf], HALF)
        out, into = 4 * dl + dx, 4 * dl + (4 - dx) % 4
        return remote(
            re[hf].at[0, 0, rows], re[hf].at[0, into, rows], ag_send.at[hf, out],
            ag_recv.at[hf, into], chip(dx, dl),
        )

    def c2_copy(hf):
        rows = pl.ds(LEAD[hf], HALF)
        return remote(
            re[hf].at[0, :, rows], re[hf].at[1, :, rows], c2_send.at[hf], c2_recv.at[hf], core
        )

    f32, bf16 = jnp.float32, jnp.bfloat16

    def forward(hf, dn):
        lhs = xe[0:SIZE[0]] if hf == 0 else xe[SIZE[0]:]
        for dl in (1, 0):
            for mr in range(4 * dl, 4 * dl + 4):
                y = lax.dot_general(
                    lhs, dn[mr * 256:(mr + 1) * 256, :], (((1,), (1,)), ((), ())),
                    preferred_element_type=f32,
                )
                if hf == 0:
                    w = y[0:PAD]
                    wray[mr] = w
                    mine[hf][mr, 0:PAD] = w[:, :BLK]
                    c1s[hf][mr, 0:PAD] = split3(w[:, BLK:])
                diff = y[LEAD[hf]:] - wray[mr, 0:1]
                mine[hf][mr, LEAD[hf]:] = diff[:, :BLK]
                c1s[hf][mr, LEAD[hf]:] = diff[:, BLK:].astype(bf16)
            c1_copy(hf, dl).start()

    def backward(hf, dn):
        lead = LEAD[hf]
        at = SIZE[0] if hf else PAD
        for n in range(4):
            cols = slice(n * 256, (n + 1) * 256)
            acc = jnp.zeros((SIZE[hf], 256), f32)
            for mr in range(CHIPS):
                lhs = jnp.concatenate([re[hf][0, mr], re[hf][1, mr]], axis=1)
                acc += jnp.dot(lhs, dn[mr * 256:(mr + 1) * 256, cols], preferred_element_type=f32)
            if hf == 0:
                wpix[:, cols] = acc[0:8]
            mine_rows = slice(hf * HALF, (hf + 1) * HALF)
            new = out_ref[mine_rows, cols] + 0.9 * acc[lead:] / wpix[0:1, cols]
            out_ref[mine_rows, cols] = new
            xe[at:at + HALF, cols] = new.astype(bf16)

    def stage_b(hf, dn):
        c2_copy(hf).wait()
        backward(hf, dn)

    def rows_sum(v):
        return jnp.sum(v.astype(f32), axis=0, keepdims=True)

    def stage_s(hf):
        lead = LEAD[hf]
        c1_copy(hf, 1).wait_recv()
        c1_copy(hf, 0).wait_recv()
        for dx, dl in FAR + ((0, 0),):
            mr = 4 * dl + dx
            data = mine[hf][mr, lead:] + c1r[hf][mr, lead:].astype(f32)
            if mr:
                rss[hf][mr, lead:] = data.astype(bf16)
            else:
                loc[hf][lead:] = data
            if hf == 0:
                w = mine[hf][mr, 0:PAD] + rows_sum(c1r[hf][mr, 0:PAD])
                if mr:
                    rss[hf][mr, 0:PAD] = split3(w)
                else:
                    loc[hf][0:PAD] = w
            if mr:
                rs_copy(hf, dx, dl).start()

    def stage_r(hf, step):
        lead = LEAD[hf]
        total = loc[hf][lead:]
        for dx, dl in reversed(FAR):
            into = 4 * dl + (4 - dx) % 4
            rs_copy(hf, dx, dl).wait_recv()
            total += rsx[hf][into, lead:].astype(f32)
        if hf == 0:
            w = rsx[hf][1, 0:PAD].astype(f32)
            for mr in range(2, CHIPS):
                w += rsx[hf][mr, 0:PAD].astype(f32)
            wtot[...] = loc[hf][0:PAD] + jnp.sum(w, axis=0, keepdims=True)
        measured = pm[step, hf * HALF:(hf + 1) * HALF]
        re[hf][0, 0, lead:] = ((measured - 1.0) - total / wtot[0:1]).astype(bf16)
        for dx, dl in FAR:
            ag_copy(hf, dx, dl).start()

    def stage_g(hf):
        for dx, dl in FAR:
            ag_copy(hf, dx, dl).wait_recv()
        c2_copy(hf).start()
        for dl in range(2):
            c1_copy(hf, dl).wait_send()
        for dx, dl in FAR:
            rs_copy(hf, dx, dl).wait_send()
            ag_copy(hf, dx, dl).wait_send()

    out_ref[...] = vol_ref[...]
    xe[0:PAD] = jnp.ones((PAD, PIXELS), bf16)
    xe[PAD:] = vol_ref[...].astype(bf16)
    re[0][:, :, 0:PAD] = jnp.ones((2, CHIPS, PAD, BLK), bf16)
    pm[0] = proj_ref[proj_rows(0)]
    assemble(0)

    forward(0, dense.at[0])
    pm_copy(2).start()
    stage_s(0)
    forward(1, dense.at[0])
    stage_s(1)
    stage_r(0, 0)
    stage_g(0)
    tile_point(1)
    assemble(1)
    tile_point(2)

    def period(step, _):
        dn, before = dense.at[step % 3], dense.at[(step + 2) % 3]
        stage_b(0, before)
        forward(0, dn)
        stage_r(1, step - 1)
        stage_s(0)
        for slot in range(EARLY, STEPS):
            @pl.when(step == slot - 1)
            def _():
                assemble(slot)
        stage_g(1)
        stage_b(1, before)
        forward(1, dn)
        pm_copy(step).wait_recv()
        stage_r(0, step)
        stage_s(1)
        stage_g(0)
        @pl.when(step + 2 < STEPS)
        def _():
            pm_copy(step + 2).start()
        for slot in range(2, EARLY):
            @pl.when(step == slot - 1)
            def _():
                if slot < 5:
                    tile_point(slot + 1)
                assemble(slot)
        return 0

    lax.fori_loop(1, STEPS, period, 0)

    last = dense.at[(STEPS - 1) % 3]
    stage_b(0, last)
    stage_r(1, STEPS - 1)
    stage_g(1)
    stage_b(1, last)

    tile_drain()
    for slot in range(1, STEPS):
        inv_copy_to(slot).wait_send()
        pm_copy(slot).wait_send()


def per_device(start_volume, tiles, pattern, projections):
    entry = jnp.arange(8, dtype=jnp.int32)[None, :, None]
    name = jnp.arange(BLK, dtype=jnp.int32)[None, None, :]
    inverse = jnp.min(jnp.where(pattern[0][:, :, None] == name, entry, 8), axis=1)
    vmem = pl.BlockSpec(memory_space=pltpu.VMEM)
    bf16, f32, i32 = jnp.bfloat16, jnp.float32, jnp.int32
    dma = pltpu.SemaphoreType.DMA
    out = pl.pallas_call(
        kernel,
        out_shape=jax.ShapeDtypeStruct((COLS, PIXELS), f32),
        in_specs=[
            vmem, pl.BlockSpec(memory_space=pl.ANY), vmem,
            pl.BlockSpec(memory_space=pltpu.SMEM), vmem,
        ],
        out_specs=vmem,
        scratch_shapes=[
            [pltpu.VMEM((8, 8, BLK, BLK), bf16)] * STEPS,
            pltpu.VMEM((STEPS, 8, BLK), i32),
            pltpu.SMEM((STEPS, 8, BLK), i32),
            pltpu.VMEM((STEPS, COLS, BLK), f32),
            pltpu.VMEM((3, RAYS, PIXELS), bf16),
            pltpu.VMEM((ROWS, PIXELS), bf16),
            pltpu.VMEM((CHIPS, PAD, 2 * BLK), f32),
            pltpu.VMEM((PAD, BLK), f32),
            pltpu.VMEM((8, PIXELS), f32),
            [pltpu.VMEM((CHIPS, n, BLK), f32) for n in SIZE],
            [pltpu.VMEM((CHIPS, n, BLK), bf16) for n in SIZE],
            [pltpu.VMEM((CHIPS, n, BLK), bf16) for n in SIZE],
            [pltpu.VMEM((CHIPS, n, BLK), bf16) for n in SIZE],
            [pltpu.VMEM((CHIPS, n, BLK), bf16) for n in SIZE],
            [pltpu.VMEM((n, BLK), f32) for n in SIZE],
            [pltpu.VMEM((2, CHIPS, n, BLK), bf16) for n in SIZE],
            dma, dma((STEPS,)), dma((STEPS,)), dma, dma((STEPS,)), dma((STEPS,)),
            dma((18,)), dma((STEPS, 2)),
            dma((2, 2)), dma((2, 2)), dma((2, CHIPS)), dma((2, CHIPS)),
            dma((2, CHIPS)), dma((2, CHIPS)), dma((2,)), dma((2,)),
        ],
        compiler_params=pltpu.CompilerParams(
            collective_id=0, has_side_effects=True, vmem_limit_bytes=56 * 2**20
        ),
        cost_estimate=pl.CostEstimate(
            flops=STEPS * 4 * RAYS * PIXELS * COLS, bytes_accessed=6 * 2**20, transcendentals=0
        ),
        name="sweep",
    )(start_volume.T, tiles[0], inverse, inverse, projections[0].T)
    return out.T


def solution(mesh):
    in_specs = (
        P("tile", "subset"),
        P("subset", "tile", None, None, None),
        P("subset", "tile", None),
        P("subset", "tile", None),
    )
    return jax.shard_map(
        per_device, mesh=mesh, in_specs=in_specs, out_specs=P("tile", "subset"), check_vma=False
    )
```

time: 1260 us -> 265 us (0.21)
  waiting for transfers between devices: 960 us -> 0 us
  Pallas kernels: 0 us -> 257 us
  other arithmetic: 125 us -> 1.46 us
  matrix products: 60.8 us -> 0 us
  local copies, waits for them, and re-layouts: 50.2 us -> 6.39 us
  blocking collectives: 28.5 us -> 0 us
  starting transfers between devices: 20.2 us -> 0 us
  between operations: 13.1 us -> 0.01 us
    reduce_scatter x8 -> x0, waiting for transfers between devices: 475 us -> none  [update(): lax.psum_scatter(partial_sums, 'tile', scatter_dimension=0, tiled=True)]
    all_gather x8 -> x0, waiting for transfers between devices: 278 us -> none  [update(): residual_all = lax.all_gather(residual, 'tile', axis=0, tiled=True)]
    pallas_call x0 -> x1, Pallas kernels: none -> 257 us  [per_device(): pl.pallas_call(kernel, out_shape=jax.ShapeDtypeStruct((COLS, PIXELS), f32...]
    ppermute x8 -> x0, waiting for transfers between devices: 207 us -> none  [passed_along(): lax.ppermute(value, axis, [(i, (i + by) % devices) for i in range(devices)])]
    scatter-add x9 -> x0, other arithmetic: 101 us -> none  [the longest x8 99.8 us: update(): partial_sums = jnp.zeros((ray_blocks, block, width), jnp.float32).at[flat...]
    dot_general x16 -> x0, matrix products: 60.8 us -> none  [the longest x8 36.2 us: update(): jnp.einsum('qkrp,qps->qkrs', tile_set, image, preferred_element_type=jnp....]
    gather x8 -> x0, local copies, waits for them, and re-layouts: 31.7 us -> none  [update(): chosen = residual_all[links]]
    unnamed x1 -> x0, blocking collectives: 28.5 us -> none
  transfers between devices with their start and end apart: 24 -> 0, of which waited for: 24 -> 0; matrix products, arithmetic and copies ran while one was open for 0% -> 0% of each run, Pallas kernels for 0% -> 0%
where the time goes in v2:
time: 265 us
  Pallas kernels  257 us (97%)
  local copies, waits for them, and re-layouts  6.39 us (2%)
    pallas_call x1, Pallas kernels, per_device(): pl.pallas_call(kernel, out_shape=jax.ShapeDtypeStruct((COLS, PIXELS), f32...  257 us

profile of v2, /device:TPU:1, one launch (start us, length us, event | category | flops | bytes accessed | tf_op | source)
XLA Modules:
  0.0 264.6 jit_solution(9688573128458732569)
XLA Ops:
  0.0 0.0 copy-start
  0.0 1.5 select_reduce_fusion.inv_ref.inv0_ref
  1.5 2.5 copy.8
  4.0 0.0 copy-done
  4.0 1.3 copy.9
  5.3 256.7 %sweep.1 = f32[256,1024]{1,0:T(8,128)} custom-call(f32[256,1024]{1,0:T(8,128)} %bitcast.8, bf16[8,8,128,128]{3,2,1,0:T(8,128)(2,1)} %bitcast.11, s32[8,128]{1,0:T(8,128)} %select_reduce_fusion.inv_ref.inv0_ref, s32[8,128]{1,0:T(8,128)} %select_reduce_fusion.inv_ref.inv0_ref, f32[2048,128]{1,0:T(8,128)} %bitcast.9), custom_call_target="tpu_custom_call" | custom-call | flops 17179869184 | bytes 6291456 | tf_op jit(solution)/shard_map/sweep/pallas_call | solution.py:370
  262.0 2.5 copy.10
Async XLA Ops:
  0.0 4.0 %copy-start = (f32[1,128,2048]{2,1,0:T(8,128)S(1)}, f32[1,128,2048]{2,1,0:T(8,128)}, u32[]{:S(2)}) copy-start(f32[1,128,2048]{2,1,0:T(8,128)} %param.7) | copy-start | bytes 3145732

commit v3 on v2

--- a/solution.py
+++ b/solution.py
@@ -9,7 +9,7 @@
 BLK = 128
 STEPS = 8
 CHIPS = 8
-EARLY = 6
+EARLY = 4
 COLS = 256
 PAD = 16
 ROWS = COLS + PAD
@@ -31,7 +31,7 @@
 
 
 def kernel(
-    vol_ref, tile_ref, inv_ref, inv0_ref, proj_ref, out_ref,
+    vol_ref, tile_ref, pat_ref, proj_ref, out_ref,
     tb, inv_v, inv_s, pm, dense, xe, wray, wtot, wpix, mine, c1s, c1r, rss, rsx, loc, re,
     tile_sem, inv_send, inv_recv, inv_copy, pm_send, pm_recv, t_send, t_recv,
     c1_send, c1_recv, rs_send, rs_recv, ag_send, ag_recv, c2_send, c2_recv,
@@ -71,62 +71,78 @@
     pl.semaphore_wait(barrier, len(partners))
     own.wait()
 
-    def piece(slot, p):
-        return tb[slot].at[pl.ds(4 * p, 4)]
-
-    def tile_copy(idx, src, p, dst, device):
-        return remote(piece(src, p), piece(dst, p), t_send.at[idx], t_recv.at[dst, p], device)
+    def piece(slot, q, n):
+        return tb[slot].at[pl.ds(q, n)]
+
+    def tile_copy(idx, src, q, n, dst, device):
+        return remote(
+            piece(src, q, n), piece(dst, q, n), t_send.at[idx], t_recv.at[dst, q // 2], device
+        )
 
     flows = (
         (
-            (("-", 0, 0, 2), ("+", 0, 0, 6), ("y", 0, 1, 7)),
-            (("-", 0, 1, 2), ("+", 6, 0, 4), ("y", 2, 0, 1)),
-            (("-", 1, 1, 3), ("+", 0, 1, 6), ("y", 0, 0, 7)),
-            (("-", 1, 0, 3), ("+", 1, 0, 7)),
-            (("-", 2, 1, 4), ("+", 7, 0, 5)),
-            (("-", 3, 1, 5), ("+", 1, 1, 7)),
+            (("-", 0, 0, 2, 2), ("+", 0, 0, 4, 6), ("y", 0, 4, 2, 7)),
+            (("-", 0, 2, 2, 2), ("y", 0, 6, 2, 7)),
+            (("-", 0, 4, 4, 2), ("y", 2, 0, 2, 1)),
+            (("y", 2, 2, 2, 1), ("+", 6, 0, 4, 4), ("-", 1, 4, 4, 3)),
+            (("-", 1, 0, 4, 3), ("+", 0, 4, 4, 6), ("y", 0, 0, 4, 7)),
+            (("-", 2, 4, 4, 4), ("+", 1, 0, 4, 7)),
+            (("-", 3, 4, 4, 5), ("+", 7, 0, 4, 5)),
+            (("+", 1, 4, 4, 7),),
         ),
         (
-            (("-", 0, 0, 2), ("+", 0, 0, 6), ("y", 0, 1, 1)),
-            (("-", 7, 1, 1), ("+", 7, 1, 5), ("y", 0, 0, 1)),
-            (("-", 0, 1, 2), ("+", 5, 1, 3)),
-            (("-", 1, 0, 3), ("+", 0, 1, 6)),
-            (("-", 2, 0, 4), ("+", 6, 1, 4)),
-            (("+", 7, 0, 5),),
+            (("-", 0, 0, 2, 2), ("+", 0, 0, 4, 6), ("y", 0, 4, 2, 1)),
+            (("-", 0, 2, 2, 2), ("y", 0, 6, 2, 1)),
+            (("-", 7, 4, 2, 1), ("+", 7, 4, 2, 5), ("y", 0, 0, 2, 1)),
+            (("-", 7, 6, 2, 1), ("y", 0, 2, 2, 1), ("+", 7, 6, 2, 5), ("-", 0, 4, 4, 2)),
+            (("-", 1, 0, 4, 3), ("+", 5, 4, 4, 3)),
+            (("-", 2, 4, 4, 4), ("+", 6, 0, 4, 4)),
+            (("+", 7, 0, 4, 5),),
+            (("+", 0, 4, 4, 6),),
         ),
     )
-    events = [("send", 0), ("send", 1), ("make", 1), ("send", 2)]
+    events = [("send", 0), ("send", 1), ("send", 2), ("send", 3), ("make", 1), ("send", 4)]
     for slot in range(2, STEPS):
-        if slot + 1 < len(flows[0]):
-            events.append(("send", slot + 1))
-        events.append(("make", slot))
+        sends = [("send", slot + 3)] if slot + 3 < len(flows[0]) else []
+        make = [("make", slot)]
+        events += make + sends if slot >= EARLY else sends + make
     waits = ({}, {})
     for row in range(2):
-        seen = set()
+        coming = []
+        for other in range(2):
+            for point in flows[other]:
+                for way, _, q, n, dst in point:
+                    if (way == "y") == (other != row):
+                        coming.append((dst, q, n))
         for kind, at in events:
             if kind == "send":
-                reads = sorted({(src, p) for _, src, p, _ in flows[row][at] if src})
+                reads = [(src, q, n) for _, src, q, n, _ in flows[row][at]]
             else:
-                reads = [(at, 0), (at, 1)]
-            waits[row][kind, at] = [r for r in reads if r not in seen]
-            seen.update(reads)
+                reads = [(at, 0, 8)]
+            waits[row][kind, at] = []
+            for piece_in in tuple(coming):
+                slot, q, n = piece_in
+                if any(slot == s and q < p + m and p < q + n for s, p, m in reads):
+                    waits[row][kind, at].append(piece_in)
+                    coming.remove(piece_in)
 
     def tile_arrived(row, kind, at):
-        for slot, p in waits[row][kind, at]:
-            tile_copy(0, slot, p, slot, y_dev).wait_recv()
+        for slot, q, n in waits[row][kind, at]:
+            tile_copy(0, slot, q, n, slot, y_dev).wait_recv()
 
     def flow_copies(row, point):
-        for i, (way, src, p, dst) in enumerate(flows[row][point]):
+        for i, (way, src, q, n, dst) in enumerate(flows[row][point]):
             device = y_dev if way == "y" else z_dev[-1 if way == "-" else 1]
-            yield tile_copy(3 * point + i, src, p, dst, device)
+            yield tile_copy(4 * point + i, src, q, n, dst, device)
 
     def tile_point(point):
         for row in range(2):
-            @pl.when(h == row)
-            def _():
-                tile_arrived(row, "send", point)
-                for copy in flow_copies(row, point):
-                    copy.start()
+            if flows[row][point]:
+                @pl.when(h == row)
+                def _():
+                    tile_arrived(row, "send", point)
+                    for copy in flow_copies(row, point):
+                        copy.start()
 
     def tile_drain():
         for row in range(2):
@@ -142,39 +158,45 @@
             def _():
                 tile_arrived(row, "make", slot)
 
-    def proj_rows(d):
-        return pl.ds(pl.multiple_of(((c + d) % STEPS) * COLS, COLS), COLS)
+    def proj_cols(d):
+        return slice(None), pl.ds(pl.multiple_of(((c + d) % STEPS) * COLS, COLS), COLS)
 
     def pm_copy(slot):
         d = STEPS - slot
         return remote(
-            proj_ref.at[proj_rows(d)], pm.at[slot], pm_send.at[slot], pm_recv.at[slot], group(d)
+            proj_ref.at[proj_cols(d)], pm.at[slot], pm_send.at[slot], pm_recv.at[slot], group(d)
         )
 
     def inv_copy_to(slot):
         return remote(
-            inv_ref, inv_v.at[slot], inv_send.at[slot], inv_recv.at[slot], group(STEPS - slot)
-        )
-
+            inv_v.at[0], inv_v.at[slot], inv_send.at[slot], inv_recv.at[slot], group(STEPS - slot)
+        )
+
+    tile_point(0)
+    name = lax.broadcasted_iota(jnp.int32, (8, BLK), 1)
+    inverse = jnp.full((8, BLK), 8, jnp.int32)
+    for entry in range(8):
+        inverse = jnp.where(pat_ref[:, entry:entry + 1] == name, entry, inverse)
+    inv_v[0] = inverse
     for slot in range(1, STEPS):
         inv_copy_to(slot).start()
     pm_copy(1).start()
-    tile_point(0)
 
     def assemble(slot):
         dn = dense.at[slot % 3]
         if slot:
             inv_copy_to(slot).wait_recv()
-            local = pltpu.make_async_copy(inv_v.at[slot], inv_s.at[slot], inv_copy)
-            local.start()
-            local.wait()
+        local = pltpu.make_async_copy(inv_v.at[slot], inv_s.at[slot], inv_copy)
+        local.start()
+        local.wait()
+        if slot:
             tile_wait(slot)
 
         def block(i, _):
             mr, j = i // 2, i % 2
             b = (((x + mr % 4) % 4) * 2 + (l + mr // 4) % 2) * 2 + (k + j) % 2
             for q in range(8):
-                at = inv_s[slot, q, b] if slot else inv0_ref[q, b]
+                at = inv_s[slot, q, b]
                 tile = tb[slot][q, jnp.minimum(at, 7)]
                 dn[pl.ds(pl.multiple_of(i * BLK, BLK), BLK), q * BLK:(q + 1) * BLK] = jnp.where(
                     at < 8, tile, jnp.zeros_like(tile)
@@ -275,6 +297,7 @@
 
     def stage_r(hf, step):
         lead = LEAD[hf]
+        measured = pm[step, :, hf * HALF:(hf + 1) * HALF].T - 1.0
         total = loc[hf][lead:]
         for dx, dl in reversed(FAR):
             into = 4 * dl + (4 - dx) % 4
@@ -285,8 +308,7 @@
             for mr in range(2, CHIPS):
                 w += rsx[hf][mr, 0:PAD].astype(f32)
             wtot[...] = loc[hf][0:PAD] + jnp.sum(w, axis=0, keepdims=True)
-        measured = pm[step, hf * HALF:(hf + 1) * HALF]
-        re[hf][0, 0, lead:] = ((measured - 1.0) - total / wtot[0:1]).astype(bf16)
+        re[hf][0, 0, lead:] = (measured - total / wtot[0:1]).astype(bf16)
         for dx, dl in FAR:
             ag_copy(hf, dx, dl).start()
 
@@ -300,11 +322,12 @@
             rs_copy(hf, dx, dl).wait_send()
             ag_copy(hf, dx, dl).wait_send()
 
-    out_ref[...] = vol_ref[...]
+    for n in range(4):
+        out_ref[:, n * 256:(n + 1) * 256] = vol_ref[n * 256:(n + 1) * 256, :].T
     xe[0:PAD] = jnp.ones((PAD, PIXELS), bf16)
-    xe[PAD:] = vol_ref[...].astype(bf16)
+    xe[PAD:] = out_ref[...].astype(bf16)
     re[0][:, :, 0:PAD] = jnp.ones((2, CHIPS, PAD, BLK), bf16)
-    pm[0] = proj_ref[proj_rows(0)]
+    pm[0] = proj_ref[proj_cols(0)]
     assemble(0)
 
     forward(0, dense.at[0])
@@ -312,11 +335,13 @@
     stage_s(0)
     forward(1, dense.at[0])
     stage_s(1)
+    tile_point(1)
     stage_r(0, 0)
     stage_g(0)
-    tile_point(1)
+    tile_point(2)
+    tile_point(3)
     assemble(1)
-    tile_point(2)
+    tile_point(4)
 
     def period(step, _):
         dn, before = dense.at[step % 3], dense.at[(step + 2) % 3]
@@ -338,12 +363,14 @@
         @pl.when(step + 2 < STEPS)
         def _():
             pm_copy(step + 2).start()
-        for slot in range(2, EARLY):
-            @pl.when(step == slot - 1)
-            def _():
-                if slot < 5:
-                    tile_point(slot + 1)
-                assemble(slot)
+        for slot in range(2, STEPS):
+            if slot < EARLY or slot + 3 < len(flows[0]):
+                @pl.when(step == slot - 1)
+                def _():
+                    if slot + 3 < len(flows[0]):
+                        tile_point(slot + 3)
+                    if slot < EARLY:
+                        assemble(slot)
         return 0
 
     lax.fori_loop(1, STEPS, period, 0)
@@ -361,9 +388,6 @@
 
 
 def per_device(start_volume, tiles, pattern, projections):
-    entry = jnp.arange(8, dtype=jnp.int32)[None, :, None]
-    name = jnp.arange(BLK, dtype=jnp.int32)[None, None, :]
-    inverse = jnp.min(jnp.where(pattern[0][:, :, None] == name, entry, 8), axis=1)
     vmem = pl.BlockSpec(memory_space=pltpu.VMEM)
     bf16, f32, i32 = jnp.bfloat16, jnp.float32, jnp.int32
     dma = pltpu.SemaphoreType.DMA
@@ -371,15 +395,14 @@
         kernel,
         out_shape=jax.ShapeDtypeStruct((COLS, PIXELS), f32),
         in_specs=[
-            vmem, pl.BlockSpec(memory_space=pl.ANY), vmem,
-            pl.BlockSpec(memory_space=pltpu.SMEM), vmem,
+            vmem, pl.BlockSpec(memory_space=pl.ANY), vmem, vmem,
         ],
         out_specs=vmem,
         scratch_shapes=[
             [pltpu.VMEM((8, 8, BLK, BLK), bf16)] * STEPS,
             pltpu.VMEM((STEPS, 8, BLK), i32),
             pltpu.SMEM((STEPS, 8, BLK), i32),
-            pltpu.VMEM((STEPS, COLS, BLK), f32),
+            pltpu.VMEM((STEPS, BLK, COLS), f32),
             pltpu.VMEM((3, RAYS, PIXELS), bf16),
             pltpu.VMEM((ROWS, PIXELS), bf16),
             pltpu.VMEM((CHIPS, PAD, 2 * BLK), f32),
@@ -393,7 +416,7 @@
             [pltpu.VMEM((n, BLK), f32) for n in SIZE],
             [pltpu.VMEM((2, CHIPS, n, BLK), bf16) for n in SIZE],
             dma, dma((STEPS,)), dma((STEPS,)), dma, dma((STEPS,)), dma((STEPS,)),
-            dma((18,)), dma((STEPS, 2)),
+            dma((32,)), dma((STEPS, 4)),
             dma((2, 2)), dma((2, 2)), dma((2, CHIPS)), dma((2, CHIPS)),
             dma((2, CHIPS)), dma((2, CHIPS)), dma((2,)), dma((2,)),
         ],
@@ -404,7 +427,7 @@
             flops=STEPS * 4 * RAYS * PIXELS * COLS, bytes_accessed=6 * 2**20, transcendentals=0
         ),
         name="sweep",
-    )(start_volume.T, tiles[0], inverse, inverse, projections[0].T)
+    )(start_volume, tiles[0], pattern[0], projections[0])
     return out.T
 
 

time: 265 us -> 255 us (0.962)
  Pallas kernels: 257 us -> 253 us
  local copies, waits for them, and re-layouts: 6.39 us -> 2.53 us
    pallas_call x1, Pallas kernels: 257 us -> 253 us  [per_device(): pl.pallas_call(kernel, out_shape=jax.ShapeDtypeStruct((COLS, PIXELS), f32...]
    unnamed x4 -> x0, local copies, waits for them, and re-layouts: 3.86 us -> none
where the time goes in v3:
time: 255 us
  Pallas kernels  253 us (99%)
    pallas_call x1, Pallas kernels, per_device(): pl.pallas_call(kernel, out_shape=jax.ShapeDtypeStruct((COLS, PIXELS), f32...  253 us

profile of v3, /device:TPU:1, one launch (start us, length us, event | category | flops | bytes accessed | tf_op | source)
XLA Modules:
  0.0 255.1 jit_solution(4834770413810034485)
XLA Ops:
  0.0 252.6 %sweep.1 = f32[256,1024]{1,0:T(8,128)} custom-call(f32[1024,256]{1,0:T(8,128)} %vol_ref.1, bf16[8,8,128,128]{3,2,1,0:T(8,128)(2,1)} %bitcast.5, s32[8,8]{1,0:T(8,128)} %bitcast.7, f32[128,2048]{1,0:T(8,128)} %bitcast.6), custom_call_target="tpu_custom_call" | custom-call | flops 17179869184 | bytes 6291456 | tf_op jit(solution)/shard_map/sweep/pallas_call | solution.py:394
  252.6 2.5 copy.5

commit v4 on v3

--- a/solution.py
+++ b/solution.py
@@ -346,8 +346,8 @@
     def period(step, _):
         dn, before = dense.at[step % 3], dense.at[(step + 2) % 3]
         stage_b(0, before)
+        stage_r(1, step - 1)
         forward(0, dn)
-        stage_r(1, step - 1)
         stage_s(0)
         for slot in range(EARLY, STEPS):
             @pl.when(step == slot - 1)
@@ -355,9 +355,9 @@
                 assemble(slot)
         stage_g(1)
         stage_b(1, before)
-        forward(1, dn)
         pm_copy(step).wait_recv()
         stage_r(0, step)
+        forward(1, dn)
         stage_s(1)
         stage_g(0)
         @pl.when(step + 2 < STEPS)

time: 255 us -> 243 us (0.953)
  Pallas kernels: 253 us -> 241 us
    pallas_call x1, Pallas kernels: 253 us -> 241 us  [per_device(): pl.pallas_call(kernel, out_shape=jax.ShapeDtypeStruct((COLS, PIXELS), f32...]
where the time goes in v4:
time: 243 us
  Pallas kernels  241 us (99%)
  local copies, waits for them, and re-layouts  2.53 us (1%)
    pallas_call x1, Pallas kernels, per_device(): pl.pallas_call(kernel, out_shape=jax.ShapeDtypeStruct((COLS, PIXELS), f32...  241 us

profile of v4, /device:TPU:1, one launch (start us, length us, event | category | flops | bytes accessed | tf_op | source)
XLA Modules:
  0.0 243.1 jit_solution(7911756202072145450)
XLA Ops:
  0.0 240.5 %sweep.1 = f32[256,1024]{1,0:T(8,128)} custom-call(f32[1024,256]{1,0:T(8,128)} %vol_ref.1, bf16[8,8,128,128]{3,2,1,0:T(8,128)(2,1)} %bitcast.5, s32[8,8]{1,0:T(8,128)} %bitcast.7, f32[128,2048]{1,0:T(8,128)} %bitcast.6), custom_call_target="tpu_custom_call" | custom-call | flops 17179869184 | bytes 6291456 | tf_op jit(solution)/shard_map/sweep/pallas_call | solution.py:394
  240.5 2.5 %copy.5 = f32[1024,256]{1,0:T(8,128)} copy(f32[1024,256]{0,1:T(8,128)} %bitcast.4) | data formatting | bytes 2097152 | tf_op jit(solution)/shard_map/transpose | solution.py:431
